TPU v7x, 512 devices: a whole 4x8x8 slice. The times are simulated.
512 devices in a mesh: section: 16 (over y, core), tensor: 32 (over x, z).
Axes of the slice: x: 4, y: 8, z: 8, core: 2. Of those that a mesh axis runs over, the one named last changes fastest.
Arguments:
- carry_in: bfloat16 [16, 2, 64, 4096], P('section', None, 'tensor'), may hold values from -6 to 6
- norm_gain: float32 [16, 4096], P('section'), may hold values from 0.5 to 1.5
- w_gate: bfloat16 [16, 1536, 128, 128], P('section', 'tensor'), may hold values from -0.15625 to 0.15625
- w_up: bfloat16 [16, 1536, 128, 128], P('section', 'tensor'), may hold values from -0.15625 to 0.15625
- w_down: bfloat16 [16, 1536, 128, 128], P('section', 'tensor'), may hold values from -0.078125 to 0.078125
- tile_list: int32 [16, 1536], P('section', 'tensor'), may hold values from 0 to 128, as said below
- grad_in: bfloat16 [16, 2, 64, 4096], P('section', None, 'tensor'), may hold values from -6 to 6
Outputs:
- section_out: bfloat16 [16, 2, 64, 4096], P('section', None, 'tensor')
- grad_back: bfloat16 [16, 2, 64, 4096], P('section', None, 'tensor')
Inputs may be any that keep to these rules, and one draw needn't show every extreme that they name: `tile_list`: for each layer and tensor index t, entries 48 * t to 48 * t + 47 list distinct tile numbers f * 32 + c (f a block of that device's hidden units, c a block of features) in rising order, followed by the padding value 4 * 32. Each such list has at least 24 live entries, and in every layer some tensor index has all 48 live.
All inputs are finite; a program needn't handle non-finite values.
Results may differ from a plain program's by a relative error of at most 0.013.
Values may be sent and summed in bfloat16 or wider, within the bound.
No kernel may reach another device: no remote copies, remote signals or barrier semaphores. Data moves between devices by JAX's collectives and lax.ppermute only.
A program may use at most 64 MiB of HBM per device.

v0:
```python
import jax
import jax.numpy as jnp
from jax import lax
from jax.experimental import pallas as pl
from jax.experimental.pallas import tpu as pltpu
from jax.sharding import PartitionSpec as P

EPS = 1e-05
BLK = 128
FB_DEV = 4
DBLOCKS = 32
NX = 4
NZ = 8
ROWS = 4
F32 = jnp.float32
BF16 = jnp.bfloat16

SPARSE = [[x * NZ + z for z in range(p, NZ, 2)] for x in range(NX) for p in range(2)]
DENSE = [[x * NZ + z + p for x in range(NX) for p in range(2)] for z in range(0, NZ, 2)]


def shifted(block, axis, distance):
    devices = range(lax.axis_size(axis))
    route = [((i - distance) % len(devices), i) for i in devices]
    return lax.ppermute(block, axis, route)


def rms_scale(values):
    return lax.rsqrt(jnp.mean(values * values, axis=-1, keepdims=True) + EPS)


def exchange(chunks, groups):
    return lax.all_to_all(chunks, "tensor", 0, 0, axis_index_groups=groups)


def spread(shard, groups):
    copies = jnp.broadcast_to(shard[None], (len(groups[0]),) + shard.shape)
    return exchange(copies, groups)


def collected(chunks, groups):
    return jnp.sum(exchange(chunks, groups).astype(F32), axis=0)


def dot_t(left, right):
    return lax.dot_general(left, right, (((1,), (1,)), ((), ())), preferred_element_type=F32)


def fill_pairs(ids, table):
    slots, = ids.shape
    pairs = table.shape[0] - 1
    for p in range(pairs):
        table[p] = packed(0, 0, FB_DEV, DBLOCKS, DBLOCKS)
    p = jnp.int32(-1)
    last = jnp.int32(-1)
    first = jnp.int32(0)
    first_c = jnp.int32(0)
    open_pair = jnp.bool_(False)
    for i in range(slots):
        q = ids[i]
        h = q // DBLOCKS
        c = q % DBLOCKS
        live = h < FB_DEV
        joins = jnp.logical_and(open_pair, h == last)
        p = jnp.where(joins, p, p + 1)
        first = jnp.where(joins, first, i)
        first_c = jnp.where(joins, first_c, c)
        table[jnp.where(live, p, pairs)] = packed(
            first, i, h, first_c, jnp.where(joins, c, DBLOCKS)
        )
        open_pair = jnp.logical_not(joins)
        last = h


def packed(a, b, h, ca, cb):
    return (((h * 64 + ca) * 64 + cb) * 64 + a) * 64 + b


def unpacked(word):
    return (word // 64) % 64, word % 64, word // 64**4, (word // 64**3) % 64, (word // 64**2) % 64


def layer_kernel(ids, g_ref, wg_ref, wu_ref, wd_ref, out_ref, table, xs, ds, gu, dh, hid, dgu, fo, bo):
    rows, width = g_ref.shape
    half = rows // 2
    pairs = table.shape[0] - 1
    fill_pairs(ids, table)

    row = lax.broadcasted_iota(jnp.int32, (rows, rows), 0)
    col = lax.broadcasted_iota(jnp.int32, (rows, rows), 1)

    def source(i):
        within = i % half
        return (within // ROWS) * (2 * ROWS) + within % ROWS + (i // half) * ROWS

    sort_rows = (col == source(row)).astype(BF16)
    mix_rows = (row == source(col)).astype(BF16)

    gu[...] = jnp.zeros_like(gu)
    dh[...] = jnp.zeros_like(dh)
    fo[...] = jnp.zeros_like(fo)
    bo[...] = jnp.zeros_like(bo)
    for k in range(width // (2 * BLK)):
        part = jnp.dot(
            sort_rows, g_ref[:, k * 2 * BLK : (k + 1) * 2 * BLK], preferred_element_type=F32
        ).astype(BF16)
        for i in range(2):
            xs[2 * k + i] = part[:half, i * BLK : (i + 1) * BLK]
            ds[2 * k + i] = part[half:, i * BLK : (i + 1) * BLK]
    xs[DBLOCKS] = jnp.zeros((half, BLK), BF16)
    ds[DBLOCKS] = jnp.zeros((half, BLK), BF16)

    def tiles(ref, a, b, axis):
        return jnp.concatenate([ref[a], ref[b]], axis=axis)

    def both(a, b):
        return jnp.concatenate([tiles(wg_ref, a, b, 0), tiles(wu_ref, a, b, 0)], axis=1)

    for p in range(pairs):
        a, b, h, ca, cb = unpacked(table[p])
        gu[h] += jnp.dot(tiles(xs, ca, cb, 1), both(a, b), preferred_element_type=F32)
        dh[h] += dot_t(tiles(ds, ca, cb, 1), tiles(wd_ref, a, b, 1))

    for h in range(FB_DEV):
        gate = gu[h, :, :BLK]
        up = gu[h, :, BLK:]
        sig = 1.0 / (1.0 + jnp.exp(-gate))
        hid[h] = (gate * sig * up).astype(BF16)
        d_hidden = dh[h]
        dgu[h, :, :BLK] = (d_hidden * up * sig * (1.0 + gate * (1.0 - sig))).astype(BF16)
        dgu[h, :, BLK:] = (d_hidden * gate * sig).astype(BF16)
    hid[FB_DEV] = jnp.zeros((half, BLK), BF16)
    dgu[FB_DEV] = jnp.zeros((half, 2 * BLK), BF16)

    for p in range(pairs):
        a, b, h, ca, cb = unpacked(table[p])
        forth = jnp.dot(hid[h], tiles(wd_ref, a, b, 1), preferred_element_type=F32)
        back = dot_t(dgu[h], both(a, b))
        fo[ca] += forth[:, :BLK]
        fo[cb] += forth[:, BLK:]
        bo[ca] += back[:, :BLK]
        bo[cb] += back[:, BLK:]

    for k in range(DBLOCKS // 2):
        terms = [
            jnp.concatenate([fo[i].astype(BF16), bo[i].astype(BF16)], axis=0)
            for i in (2 * k, 2 * k + 1)
        ]
        out_ref[:, k * 2 * BLK : (k + 1) * 2 * BLK] = jnp.dot(
            mix_rows, jnp.concatenate(terms, axis=1), preferred_element_type=F32
        ).astype(BF16)


def layer(ids, gathered, w_gate, w_up, w_down):
    rows, width = gathered.shape
    half = rows // 2
    dblocks = width // BLK
    vmem = pl.BlockSpec(memory_space=pltpu.VMEM)
    slots = w_gate.shape[0]
    return pl.pallas_call(
        layer_kernel,
        out_shape=jax.ShapeDtypeStruct((rows, width), BF16),
        in_specs=[pl.BlockSpec(memory_space=pltpu.SMEM), vmem, vmem, vmem, vmem],
        out_specs=vmem,
        scratch_shapes=[
            pltpu.SMEM(((slots + FB_DEV) // 2 + 1,), jnp.int32),
            pltpu.VMEM((dblocks + 1, half, BLK), BF16),
            pltpu.VMEM((dblocks + 1, half, BLK), BF16),
            pltpu.VMEM((FB_DEV + 1, half, 2 * BLK), F32),
            pltpu.VMEM((FB_DEV + 1, half, BLK), F32),
            pltpu.VMEM((FB_DEV + 1, half, BLK), BF16),
            pltpu.VMEM((FB_DEV + 1, half, 2 * BLK), BF16),
            pltpu.VMEM((dblocks + 1, half, BLK), F32),
            pltpu.VMEM((dblocks + 1, half, BLK), F32),
        ],
        compiler_params=pltpu.CompilerParams(vmem_limit_bytes=40 * 1024 * 1024),
        cost_estimate=pl.CostEstimate(
            flops=12 * slots * half * BLK * BLK,
            bytes_accessed=6 * slots * BLK * BLK + 4 * rows * width,
            transcendentals=FB_DEV * half * BLK,
        ),
    )(ids, gathered, w_gate, w_up, w_down)


def on_device(carry_in, norm_gain, w_gate, w_up, w_down, tile_list, grad_in):
    _, batches, tok_dev, width = carry_in.shape
    own = batches * tok_dev
    x_own = shifted(carry_in.reshape(own, width), "section", 1).astype(F32)
    dy_own = grad_in.reshape(own, width)
    gain = norm_gain[0]
    scale = rms_scale(x_own)
    normed = (x_own * scale * gain).astype(BF16)

    shard = jnp.concatenate([normed, dy_own], axis=0)
    gathered = spread(shard, SPARSE).reshape(-1, width)
    gathered = spread(gathered, DENSE).reshape(-1, width)

    terms = layer(tile_list[0], gathered, w_gate[0], w_up[0], w_down[0])

    sums = collected(terms.reshape(len(DENSE[0]), -1, width), DENSE).astype(BF16)
    sums = collected(sums.reshape(len(SPARSE[0]), -1, width), SPARSE)
    ffn_own = sums[:own]
    grad_normed = sums[own:]

    section_out = (x_own + ffn_own).astype(BF16)
    mixed = jnp.mean(x_own * gain * grad_normed, axis=-1, keepdims=True)
    grad_x = dy_own.astype(F32) + scale * gain * grad_normed - x_own * scale**3 * mixed
    grad_back = shifted(grad_x.astype(BF16), "section", -1)
    return (
        section_out.reshape(1, batches, tok_dev, width),
        grad_back.reshape(1, batches, tok_dev, width),
    )


def solution(mesh):
    placed = (
        P("section", None, "tensor", None),
        P("section", None),
        P("section", "tensor", None, None),
        P("section", "tensor", None, None),
        P("section", "tensor", None, None),
        P("section", "tensor"),
        P("section", None, "tensor", None),
    )
    return jax.shard_map(
        on_device,
        mesh=mesh,
        in_specs=placed,
        out_specs=(P("section", None, "tensor", None), P("section", None, "tensor", None)),
        check_vma=False,
    )
```

profile of v0, /device:TPU:17, one launch (start us, length us, event | category | flops | bytes accessed | tf_op | source)
XLA Modules:
  0.0 110.1 jit_solution(9286676884614285095)
XLA Ops:
  0.6 0.8 reshape.45
  1.4 1.9 %collective-permute-start = (bf16[4,4096]{1,0:T(4,128)(2,1)S(1)}, bf16[4,4096]{1,0:T(4,128)(2,1)S(1)}, u32[]{:S(2)}, u32[]{:S(2)}) collective-permute-start(bf16[4,4096]{1,0:T(4,128)(2,1)S(1)} %reshape.45), channel_id=1, source_target_pairs={{480,0},{0,32},{32,64},{64,96},{96,128},{128,160},{160,192},{192,2... | collective-permute-start | bytes 98312 | tf_op jit(solution)/shard_map/ppermute | solution.py:25
  3.3 0.8 reshape.46
  4.1 0.2 collective-permute-done
  4.3 0.1 fusion
  4.5 0.8 fusion.2
  5.3 18.3 %all_to_all.20 = bf16[4,8,4096]{2,1,0:T(8,128)(2,1)S(1)} all-to-all(bf16[4,8,4096]{2,1,0:T(8,128)(2,1)S(1)} %broadcast_in_dim.6), channel_id=1, replica_groups={{0,2,4,6},{1,3,5,7},{8,10,12,14},{9,11,13,15},{16,18,20,22},{17,19,21,2..., dimensions={0} | all-to-all | bytes 524288 | tf_op jit(solution)/shard_map/all_to_all | solution.py:33
  23.6 0.0 copy-start.2
  23.6 0.2 broadcast_in_dim.8
  23.9 0.0 copy-start
  23.9 0.0 copy-start.1
  23.9 0.0 copy-start.3
  23.9 31.0 %all_to_all.21 = bf16[8,32,4096]{2,1,0:T(8,128)(2,1)S(1)} all-to-all(bf16[8,32,4096]{2,1,0:T(8,128)(2,1)S(1)} %broadcast_in_dim.8), channel_id=1, replica_groups={{0,1,8,9,16,17,24,25},{2,3,10,11,18,19,26,27},{4,5,12,13,20,21,28,29},{..., dimensions={0} | all-to-all | bytes 4194304 | tf_op jit(solution)/shard_map/all_to_all | solution.py:33
  54.9 0.0 copy-done.2
  54.9 0.0 copy-done
  54.9 0.0 copy-done.1
  54.9 0.0 copy-done.3
  55.0 5.9 %shard_map.86 = bf16[256,4096]{1,0:T(8,128)(2,1)S(1)} custom-call(s32[48]{0:T(128)S(1)} %bitcast.14, bf16[256,4096]{1,0:T(8,128)(2,1)S(1)} %bitcast.9, bf16[48,128,128]{2,1,0:T(8,128)(2,1)S(1)} %bitcast.11, bf16[48,128,128]{2,1,0:T(8,128)(2,1)S(1)} %bitcast.12, bf16[48,128,128]{2,1,0:T(8,128)(2,1)S(1)} %bitcast.13), custom_call_target="tpu_custom_call" | custom-call | flops 1207959552 | bytes 8912896 | tf_op jit(solution)/shard_map/pallas_call | solution.py:160
  60.8 25.7 %all_to_all.22 = bf16[8,32,4096]{2,1,0:T(8,128)(2,1)S(1)} all-to-all(bf16[8,32,4096]{2,1,0:T(8,128)(2,1)S(1)} %bitcast.10), channel_id=1, replica_groups={{0,1,8,9,16,17,24,25},{2,3,10,11,18,19,26,27},{4,5,12,13,20,21,28,29},{..., dimensions={0} | all-to-all | bytes 4194304 | tf_op jit(solution)/shard_map/all_to_all | solution.py:33
  86.6 0.0 copy-start.4
  86.6 0.3 reduce_sum.40
  86.9 11.7 %all_to_all.23 = bf16[4,8,4096]{2,1,0:T(8,128)(2,1)S(1)} all-to-all(bf16[4,8,4096]{2,1,0:T(8,128)(2,1)S(1)} %bitcast.15), channel_id=1, replica_groups={{0,2,4,6},{1,3,5,7},{8,10,12,14},{9,11,13,15},{16,18,20,22},{17,19,21,2..., dimensions={0} | all-to-all | bytes 524288 | tf_op jit(solution)/shard_map/all_to_all | solution.py:33
  98.6 0.0 copy-done.4
  98.6 0.2 fusion.8
  98.8 0.1 fusion.6
  98.9 5.9 %collective-permute-start.1 = (bf16[4,4096]{1,0:T(4,128)(2,1)S(1)}, bf16[4,4096]{1,0:T(4,128)(2,1)S(1)}, u32[]{:S(2)}, u32[]{:S(2)}) collective-permute-start(bf16[4,4096]{1,0:T(4,128)(2,1)S(1)} %get-tuple-element.2), channel_id=1, source_target_pairs={{32,0},{64,32},{96,64},{128,96},{160,128},{192,160},{224,192},{256... | collective-permute-start | bytes 98312 | tf_op jit(solution)/shard_map/ppermute | solution.py:25
  104.8 0.6 reshape.50
  105.5 4.0 %collective-permute-done.1 = bf16[4,4096]{1,0:T(4,128)(2,1)S(1)} collective-permute-done((bf16[4,4096]{1,0:T(4,128)(2,1)S(1)}, bf16[4,4096]{1,0:T(4,128)(2,1)S(1)}, u32[]{:S(2)}, u32[]{:S(2)}) %collective-permute-start.1) | collective-permute-done | bytes 32800 | tf_op jit(solution)/shard_map/ppermute | solution.py:25
  109.4 0.6 reshape.51
  (5 shorter events, 0.1 us)
Async XLA Ops:
  1.4 2.9 %collective-permute-start = (bf16[4,4096]{1,0:T(4,128)(2,1)S(1)}, bf16[4,4096]{1,0:T(4,128)(2,1)S(1)}, u32[]{:S(2)}, u32[]{:S(2)}) collective-permute-start(bf16[4,4096]{1,0:T(4,128)(2,1)S(1)} %reshape.45), channel_id=1, source_target_pairs={{480,0},{0,32},{32,64},{64,96},{96,128},{128,160},{160,192},{192,2... | collective-permute-start | bytes 98312 | tf_op jit(solution)/shard_map/ppermute | solution.py:25
  23.6 31.3 %copy-start.2 = (bf16[1,48,128,128]{3,2,1,0:T(8,128)(2,1)S(1)}, bf16[1,48,128,128]{3,2,1,0:T(8,128)(2,1)}, u32[]{:S(2)}) copy-start(bf16[1,48,128,128]{3,2,1,0:T(8,128)(2,1)} %param.11) | copy-start | bytes 4718596
  23.9 31.1 %copy-start = (bf16[1,48,128,128]{3,2,1,0:T(8,128)(2,1)S(1)}, bf16[1,48,128,128]{3,2,1,0:T(8,128)(2,1)}, u32[]{:S(2)}) copy-start(bf16[1,48,128,128]{3,2,1,0:T(8,128)(2,1)} %param.9) | copy-start | bytes 4718596
  23.9 31.1 %copy-start.1 = (bf16[1,48,128,128]{3,2,1,0:T(8,128)(2,1)S(1)}, bf16[1,48,128,128]{3,2,1,0:T(8,128)(2,1)}, u32[]{:S(2)}) copy-start(bf16[1,48,128,128]{3,2,1,0:T(8,128)(2,1)} %param.10) | copy-start | bytes 4718596
  23.9 31.1 %copy-start.3 = (s32[1,48]{1,0:T(1,128)S(1)}, s32[1,48]{1,0:T(1,128)}, u32[]{:S(2)}) copy-start(s32[1,48]{1,0:T(1,128)} %param.12) | copy-start | bytes 580
  86.6 12.1 %copy-start.4 = (f32[1,4096]{1,0:T(1,128)S(1)}, f32[1,4096]{1,0:T(1,128)}, u32[]{:S(2)}) copy-start(f32[1,4096]{1,0:T(1,128)} %param.8) | copy-start | bytes 49156
  98.9 10.5 %collective-permute-start.1 = (bf16[4,4096]{1,0:T(4,128)(2,1)S(1)}, bf16[4,4096]{1,0:T(4,128)(2,1)S(1)}, u32[]{:S(2)}, u32[]{:S(2)}) collective-permute-start(bf16[4,4096]{1,0:T(4,128)(2,1)S(1)} %get-tuple-element.2), channel_id=1, source_target_pairs={{32,0},{64,32},{96,64},{128,96},{160,128},{192,160},{224,192},{256... | collective-permute-start | bytes 98312 | tf_op jit(solution)/shard_map/ppermute | solution.py:25
where the time goes:
time: 111 us; the launch traced here: 110 us
  blocking collectives  86.7 us (78%)
  starting transfers between devices  7.78 us (7%)
  Pallas kernels  5.86 us (5%)
  waiting for transfers between devices  4.22 us (4%)
  local copies, waits for them, and re-layouts  3.1 us (3%)
  other arithmetic  1.65 us (1%)
    all_to_all x4, blocking collectives, exchange(): return lax.all_to_all(chunks, 'tensor', 0, 0, axis_index_groups=groups)  86.7 us
    ppermute x2, starting transfers between devices, shifted(): return lax.ppermute(block, axis, route)  7.78 us
    pallas_call x1, Pallas kernels, layer(): pl.pallas_call(layer_kernel, out_shape=jax.ShapeDtypeStruct((rows, width)...  5.86 us
    ppermute x2, waiting for transfers between devices, shifted(): return lax.ppermute(block, axis, route)  4.22 us
  transfers between devices with their start and end apart: 2, of which 2 were waited for; matrix products, arithmetic and copies ran while one was open for 1% of the time, Pallas kernels for 0%

commit v1 on v0

--- a/solution.py
+++ b/solution.py
@@ -185,9 +185,11 @@
 def on_device(carry_in, norm_gain, w_gate, w_up, w_down, tile_list, grad_in):
     _, batches, tok_dev, width = carry_in.shape
     own = batches * tok_dev
-    x_own = shifted(carry_in.reshape(own, width), "section", 1).astype(F32)
-    dy_own = grad_in.reshape(own, width)
-    gain = norm_gain[0]
+    carried = shifted(carry_in, "section", 1)
+    dy_own, gain = lax.optimization_barrier(
+        (grad_in.reshape(own, width), jnp.broadcast_to(norm_gain, (own, width)))
+    )
+    x_own = lax.optimization_barrier(carried.reshape(own, width)).astype(F32)
     scale = rms_scale(x_own)
     normed = (x_own * scale * gain).astype(BF16)
 

time: 111 us -> 111 us (level)
  blocking collectives: 86.7 us -> 88.1 us
  waiting for transfers between devices: 4.22 us -> 5.47 us
  starting transfers between devices: 7.78 us -> 6.64 us
    all_to_all x4, blocking collectives: 86.7 us -> 88.1 us  [exchange(): return lax.all_to_all(chunks, 'tensor', 0, 0, axis_index_groups=groups)]
    ppermute x2, waiting for transfers between devices: 4.22 us -> 5.47 us  [shifted(): return lax.ppermute(block, axis, route)]
    ppermute x2, starting transfers between devices: 7.78 us -> 6.64 us  [shifted(): return lax.ppermute(block, axis, route)]
  transfers between devices with their start and end apart: 2 -> 2, of which waited for: 2 -> 1; matrix products, arithmetic and copies ran while one was open for 1% -> 2% of each run, Pallas kernels for 0% -> 0%
where the time goes in v1:
time: 111 us
  blocking collectives  88.1 us (79%)
  starting transfers between devices  6.64 us (6%)
  Pallas kernels  5.86 us (5%)
  waiting for transfers between devices  5.47 us (5%)
  local copies, waits for them, and re-layouts  3.07 us (3%)
    all_to_all x4, blocking collectives, exchange(): return lax.all_to_all(chunks, 'tensor', 0, 0, axis_index_groups=groups)  88.1 us
    ppermute x2, starting transfers between devices, shifted(): return lax.ppermute(block, axis, route)  6.64 us
    pallas_call x1, Pallas kernels, layer(): pl.pallas_call(layer_kernel, out_shape=jax.ShapeDtypeStruct((rows, width)...  5.86 us
    ppermute x2, waiting for transfers between devices, shifted(): return lax.ppermute(block, axis, route)  5.47 us
  transfers between devices with their start and end apart: 2, of which 1 were waited for; matrix products, arithmetic and copies ran while one was open for 2% of the time, Pallas kernels for 0%

profile of v1, /device:TPU:17, one launch (start us, length us, event | category | flops | bytes accessed | tf_op | source)
XLA Modules:
  0.0 110.9 jit_solution(4939155867631704059)
XLA Ops:
  0.6 1.9 %collective-permute-start = (bf16[1,2,2,4096]{3,2,1,0:T(2,128)(2,1)}, bf16[1,2,2,4096]{3,2,1,0:T(2,128)(2,1)S(1)}, u32[]{:S(2)}, u32[]{:S(2)}) collective-permute-start(bf16[1,2,2,4096]{3,2,1,0:T(2,128)(2,1)} %param.7), channel_id=1, source_target_pairs={{480,0},{0,32},{32,64},{64,96},{96,128},{128,160},{160,192},{192,2... | collective-permute-start | bytes 98312 | tf_op jit(solution)/shard_map/ppermute | solution.py:25
  2.5 0.8 reshape.46
  3.3 0.7 broadcast_in_dim.11
  4.0 0.0 collective-permute-done
  4.0 0.1 fusion
  4.2 0.1 fusion.2
  4.4 18.4 %all_to_all.20 = bf16[4,8,4096]{2,1,0:T(8,128)(2,1)S(1)} all-to-all(bf16[4,8,4096]{2,1,0:T(8,128)(2,1)S(1)} %broadcast_in_dim.24), channel_id=1, replica_groups={{0,2,4,6},{1,3,5,7},{8,10,12,14},{9,11,13,15},{16,18,20,22},{17,19,21,2..., dimensions={0} | all-to-all | bytes 524288 | tf_op jit(solution)/shard_map/all_to_all | solution.py:33
  22.8 0.0 copy-start.2
  22.8 0.2 broadcast_in_dim.26
  23.0 0.0 copy-start
  23.0 0.0 copy-start.1
  23.1 0.0 copy-start.3
  23.1 31.4 %all_to_all.21 = bf16[8,32,4096]{2,1,0:T(8,128)(2,1)S(1)} all-to-all(bf16[8,32,4096]{2,1,0:T(8,128)(2,1)S(1)} %broadcast_in_dim.26), channel_id=1, replica_groups={{0,1,8,9,16,17,24,25},{2,3,10,11,18,19,26,27},{4,5,12,13,20,21,28,29},{..., dimensions={0} | all-to-all | bytes 4194304 | tf_op jit(solution)/shard_map/all_to_all | solution.py:33
  54.5 0.0 copy-done.2
  54.5 0.0 copy-done
  54.5 0.0 copy-done.1
  54.5 0.0 copy-done.3
  54.5 5.9 %shard_map.86 = bf16[256,4096]{1,0:T(8,128)(2,1)S(1)} custom-call(s32[48]{0:T(128)S(1)} %bitcast.14, bf16[256,4096]{1,0:T(8,128)(2,1)S(1)} %bitcast.9, bf16[48,128,128]{2,1,0:T(8,128)(2,1)S(1)} %bitcast.11, bf16[48,128,128]{2,1,0:T(8,128)(2,1)S(1)} %bitcast.12, bf16[48,128,128]{2,1,0:T(8,128)(2,1)S(1)} %bitcast.13), custom_call_target="tpu_custom_call" | custom-call | flops 1207959552 | bytes 8912896 | tf_op jit(solution)/shard_map/pallas_call | solution.py:160
  60.4 26.2 %all_to_all.22 = bf16[8,32,4096]{2,1,0:T(8,128)(2,1)S(1)} all-to-all(bf16[8,32,4096]{2,1,0:T(8,128)(2,1)S(1)} %bitcast.10), channel_id=1, replica_groups={{0,1,8,9,16,17,24,25},{2,3,10,11,18,19,26,27},{4,5,12,13,20,21,28,29},{..., dimensions={0} | all-to-all | bytes 4194304 | tf_op jit(solution)/shard_map/all_to_all | solution.py:33
  86.6 0.3 reduce_sum.40
  87.0 12.1 %all_to_all.23 = bf16[4,8,4096]{2,1,0:T(8,128)(2,1)S(1)} all-to-all(bf16[4,8,4096]{2,1,0:T(8,128)(2,1)S(1)} %bitcast.15), channel_id=1, replica_groups={{0,2,4,6},{1,3,5,7},{8,10,12,14},{9,11,13,15},{16,18,20,22},{17,19,21,2..., dimensions={0} | all-to-all | bytes 524288 | tf_op jit(solution)/shard_map/all_to_all | solution.py:33
  99.1 0.2 fusion.8
  99.2 0.1 fusion.6
  99.3 4.8 %collective-permute-start.1 = (bf16[4,4096]{1,0:T(4,128)(2,1)S(1)}, bf16[4,4096]{1,0:T(4,128)(2,1)S(1)}, u32[]{:S(2)}, u32[]{:S(2)}) collective-permute-start(bf16[4,4096]{1,0:T(4,128)(2,1)S(1)} %get-tuple-element.6), channel_id=1, source_target_pairs={{32,0},{64,32},{96,64},{128,96},{160,128},{192,160},{224,192},{256... | collective-permute-start | bytes 98312 | tf_op jit(solution)/shard_map/ppermute | solution.py:25
  104.1 0.6 reshape.50
  104.8 5.5 %collective-permute-done.1 = bf16[4,4096]{1,0:T(4,128)(2,1)S(1)} collective-permute-done((bf16[4,4096]{1,0:T(4,128)(2,1)S(1)}, bf16[4,4096]{1,0:T(4,128)(2,1)S(1)}, u32[]{:S(2)}, u32[]{:S(2)}) %collective-permute-start.1) | collective-permute-done | bytes 32800 | tf_op jit(solution)/shard_map/ppermute | solution.py:25
  110.2 0.6 reshape.51
  (6 shorter events, 0.1 us)
Async XLA Ops:
  0.6 3.4 %collective-permute-start = (bf16[1,2,2,4096]{3,2,1,0:T(2,128)(2,1)}, bf16[1,2,2,4096]{3,2,1,0:T(2,128)(2,1)S(1)}, u32[]{:S(2)}, u32[]{:S(2)}) collective-permute-start(bf16[1,2,2,4096]{3,2,1,0:T(2,128)(2,1)} %param.7), channel_id=1, source_target_pairs={{480,0},{0,32},{32,64},{64,96},{96,128},{128,160},{160,192},{192,2... | collective-permute-start | bytes 98312 | tf_op jit(solution)/shard_map/ppermute | solution.py:25
  22.8 31.7 %copy-start.2 = (bf16[1,48,128,128]{3,2,1,0:T(8,128)(2,1)S(1)}, bf16[1,48,128,128]{3,2,1,0:T(8,128)(2,1)}, u32[]{:S(2)}) copy-start(bf16[1,48,128,128]{3,2,1,0:T(8,128)(2,1)} %param.11) | copy-start | bytes 4718596
  23.0 31.5 %copy-start = (bf16[1,48,128,128]{3,2,1,0:T(8,128)(2,1)S(1)}, bf16[1,48,128,128]{3,2,1,0:T(8,128)(2,1)}, u32[]{:S(2)}) copy-start(bf16[1,48,128,128]{3,2,1,0:T(8,128)(2,1)} %param.9) | copy-start | bytes 4718596
  23.0 31.4 %copy-start.1 = (bf16[1,48,128,128]{3,2,1,0:T(8,128)(2,1)S(1)}, bf16[1,48,128,128]{3,2,1,0:T(8,128)(2,1)}, u32[]{:S(2)}) copy-start(bf16[1,48,128,128]{3,2,1,0:T(8,128)(2,1)} %param.10) | copy-start | bytes 4718596
  23.1 31.4 %copy-start.3 = (s32[1,48]{1,0:T(1,128)S(1)}, s32[1,48]{1,0:T(1,128)}, u32[]{:S(2)}) copy-start(s32[1,48]{1,0:T(1,128)} %param.12) | copy-start | bytes 580
  99.3 10.9 %collective-permute-start.1 = (bf16[4,4096]{1,0:T(4,128)(2,1)S(1)}, bf16[4,4096]{1,0:T(4,128)(2,1)S(1)}, u32[]{:S(2)}, u32[]{:S(2)}) collective-permute-start(bf16[4,4096]{1,0:T(4,128)(2,1)S(1)} %get-tuple-element.6), channel_id=1, source_target_pairs={{32,0},{64,32},{96,64},{128,96},{160,128},{192,160},{224,192},{256... | collective-permute-start | bytes 98312 | tf_op jit(solution)/shard_map/ppermute | solution.py:25
